TPU v7x, 32 devices: a whole 2x2x4 slice. The times are simulated.
32 devices in a mesh: dp: 8 (over y, x, core), seq: 4 (over z).
Axes of the slice: x: 2, y: 2, z: 4, core: 2. Of those that a mesh axis runs over, the one named last changes fastest.
Arguments:
- inputs: bfloat16 [16384, 1024], P(('dp', 'seq')), may hold values from -6 to 6
- cotangent: bfloat16 [16384, 1024], P(('dp', 'seq')), may hold values from -6 to 6
- target_slot: int32 [16384], P(('dp', 'seq')), may hold values from 0 to 767, as said below
- anchor_slot: int32 [16384], P(('dp', 'seq')), may hold values from 0 to 767, as said below
- sequence_start: int32 [16384], P(('dp', 'seq')), may hold values from 0 to 2047, as said below
- attention_in: float32 [1024, 3072], P(('dp', 'seq')), may hold values from -0.09375 to 0.09375
- attention_out: float32 [1024, 1024], P(('dp', 'seq')), may hold values from -1.5 to 1.5
- gate_up: float32 [1024, 5632], P(('dp', 'seq')), may hold values from -0.09375 to 0.09375
- feed_down: float32 [2816, 1024], P(('dp', 'seq')), may hold values from -0.109375 to 0.109375
- norm_gains: float32 [2, 1024], P(None, ('dp', 'seq')), may hold values from 0.5 to 8
- first_in: float32 [1024, 3072], P(('dp', 'seq')), may hold values from -0.00048828125 to 0.00048828125
- first_out: float32 [1024, 1024], P(('dp', 'seq')), may hold values from -4.5776367e-05 to 4.5776367e-05
- first_gate: float32 [1024, 5632], P(('dp', 'seq')), may hold values from -0.00048828125 to 0.00048828125
- first_down: float32 [2816, 1024], P(('dp', 'seq')), may hold values from -0.00048828125 to 0.00048828125
- first_gains: float32 [2, 1024], P(None, ('dp', 'seq')), may hold values from -0.00048828125 to 0.00048828125
- second_in: float32 [1024, 3072], P(('dp', 'seq')), may hold values from 4.094308e-09 to 1.6346096e-08
- second_out: float32 [1024, 1024], P(('dp', 'seq')), may hold values from 4.094308e-11 to 1.6346097e-10
- second_gate: float32 [1024, 5632], P(('dp', 'seq')), may hold values from 4.094308e-09 to 1.6346096e-08
- second_down: float32 [2816, 1024], P(('dp', 'seq')), may hold values from 4.094308e-09 to 1.6346096e-08
- second_gains: float32 [2, 1024], P(None, ('dp', 'seq')), may hold values from 4.094308e-09 to 1.6346096e-08
Outputs:
- outputs: bfloat16 [16384, 1024], P(('dp', 'seq'))
- input_gradient: bfloat16 [16384, 1024], P(('dp', 'seq'))
- gradient_norm: float32 [], replicated
- updated_first_in: float32 [1024, 3072], P(('dp', 'seq'))
- updated_second_in: float32 [1024, 3072], P(('dp', 'seq'))
- updated_attention_in: float32 [1024, 3072], P(('dp', 'seq'))
- updated_first_out: float32 [1024, 1024], P(('dp', 'seq'))
- updated_second_out: float32 [1024, 1024], P(('dp', 'seq'))
- updated_attention_out: float32 [1024, 1024], P(('dp', 'seq'))
- updated_first_gate: float32 [1024, 5632], P(('dp', 'seq'))
- updated_second_gate: float32 [1024, 5632], P(('dp', 'seq'))
- updated_gate_up: float32 [1024, 5632], P(('dp', 'seq'))
- updated_first_down: float32 [2816, 1024], P(('dp', 'seq'))
- updated_second_down: float32 [2816, 1024], P(('dp', 'seq'))
- updated_feed_down: float32 [2816, 1024], P(('dp', 'seq'))
- updated_first_gains: float32 [2, 1024], P(None, ('dp', 'seq'))
- updated_second_gains: float32 [2, 1024], P(None, ('dp', 'seq'))
- updated_norm_gains: float32 [2, 1024], P(None, ('dp', 'seq'))
Inputs may be any that keep to these rules, and one draw needn't show every extreme that they name: `target_slot`: A device at seq index s sends its 512 rows to the owners of seq index s: value g * 96 + q is slot q of its block for dp index g. Values on one device are distinct and the used slots of a block are its first ones. Every owner receives 512 rows in all, and in every draw some device fills all 96 slots of some block. `anchor_slot`: value j * 96 + q: the row arrives from the device at dp index j of the same seq index, from slot q of its block for this owner; it matches target_slot, and each value stands once on a device. `sequence_start`: rows of one dp index form a group of 2048 rows in seq order; the value is the group position of the first row of the row's sequence, never above the row's own position and never falling within a group. A group holds three runs: a leading and a trailing one of 1 to 511 rows each (parts of sequences cut at the group's ends), and between them one whole sequence that begins on the first device of seq and ends on the last.
All inputs are finite; a program needn't handle non-finite values.
Results may differ from a plain program's by a relative error of at most 0.02.
Values may be sent and summed in bfloat16 or wider, within the bound.
No kernel may reach another device: no remote copies, remote signals or barrier semaphores. Data moves between devices by JAX's collectives and lax.ppermute only.
A program may use at most 256 MiB of HBM per device.

v0:
```python
import jax
import jax.numpy as jnp
from jax import lax
from jax.sharding import PartitionSpec as P

D = 1024
HEAD = 64
FF = 2816
BLOCK = 512
STEP = 10


EPSILON = 1e-05
THETA = 500000.0
NEGATIVE = -1e30
BETA_FIRST = 0.9
BETA_SECOND = 0.95
ADAM_EPSILON = 1e-08
DECAY = 0.1
CLIP = 1.0


def norm_rows(values, gain_row):
    inverse = lax.rsqrt(jnp.mean(values * values, axis=1, keepdims=True) + EPSILON)
    normal = values * inverse
    return (normal * gain_row[None, :], normal, inverse)


def norm_back(upstream, normal, inverse, gain_row):
    gain_grad = jnp.sum(upstream * normal, axis=0)
    scaled = upstream * gain_row[None, :]
    return (
        inverse * (scaled - normal * jnp.mean(scaled * normal, axis=1, keepdims=True)),
        gain_grad,
    )


def rope_tables(positions, head_size):
    half_size = head_size // 2
    frequency = jnp.power(THETA, -2.0 * jnp.arange(half_size, dtype=jnp.float32) / head_size)
    angles = positions[:, None] * frequency[None, :]
    cosine_table = jnp.cos(angles)
    sine_table = jnp.sin(angles)
    return (
        jnp.concatenate([cosine_table, cosine_table], axis=1),
        jnp.concatenate([-sine_table, sine_table], axis=1),
    )


def rotate(values, cosine_table, sine_table):
    half_size = values.shape[-1] // 2
    swapped = jnp.concatenate([values[..., half_size:], values[..., :half_size]], axis=-1)
    return values * cosine_table[:, None, :] + swapped * sine_table[:, None, :]


def rotate_back(upstream, cosine_table, sine_table):
    half_size = upstream.shape[-1] // 2
    turned = upstream * sine_table[:, None, :]
    return upstream * cosine_table[:, None, :] + jnp.concatenate(
        [turned[..., half_size:], turned[..., :half_size]], axis=-1
    )


def block_scores(queries, key_block, query_index, starts, offset, block):
    scores = (
        jnp.einsum("qhd,khd->hqk", queries, key_block, preferred_element_type=jnp.float32) * 0.125
    )
    key_index = offset + jnp.arange(block, dtype=jnp.int32)
    visible = (key_index[None, :] <= query_index[:, None]) & (key_index[None, :] >= starts[:, None])
    return (jnp.where(visible[None], scores, NEGATIVE), visible)


def attend(queries, key_rows, value_rows, starts, first_row, block):
    count, heads, head_size = queries.shape
    query_index = first_row + jnp.arange(count, dtype=jnp.int32)
    lower = starts[0] // block
    upper = (first_row + count - 1) // block + 1

    def visit(block_index, carry):
        running_max, running_sum, weighted = carry
        offset = block_index * block
        key_block = lax.dynamic_slice_in_dim(key_rows, offset, block, 0)
        value_block = lax.dynamic_slice_in_dim(value_rows, offset, block, 0)
        scores, visible = block_scores(queries, key_block, query_index, starts, offset, block)
        new_max = jnp.maximum(running_max, jnp.max(scores, axis=2))
        factor = jnp.exp(running_max - new_max)
        shares = jnp.where(visible[None], jnp.exp(scores - new_max[:, :, None]), 0.0)
        running_sum = running_sum * factor + jnp.sum(shares, axis=2)
        update = jnp.einsum(
            "hqk,khd->qhd",
            shares.astype(jnp.bfloat16),
            value_block,
            preferred_element_type=jnp.float32,
        )
        weighted = weighted * jnp.transpose(factor)[:, :, None] + update
        return (new_max, running_sum, weighted)

    initial = (
        jnp.full((heads, count), NEGATIVE, jnp.float32),
        jnp.zeros((heads, count), jnp.float32),
        jnp.zeros((count, heads, head_size), jnp.float32),
    )
    running_max, running_sum, weighted = lax.fori_loop(lower, upper, visit, initial)
    attended = weighted / jnp.transpose(running_sum)[:, :, None]
    return (attended, running_max + jnp.log(running_sum))


def attend_back(
    queries, key_rows, value_rows, starts, first_row, block, grad_heads, log_total, delta
):
    count, heads, head_size = queries.shape
    group = key_rows.shape[0]
    query_index = first_row + jnp.arange(count, dtype=jnp.int32)
    lower = starts[0] // block
    upper = (first_row + count - 1) // block + 1

    def visit(block_index, carry):
        offset = block_index * block
        key_block = lax.dynamic_slice_in_dim(key_rows, offset, block, 0)
        value_block = lax.dynamic_slice_in_dim(value_rows, offset, block, 0)
        scores, visible = block_scores(queries, key_block, query_index, starts, offset, block)
        shares = jnp.where(visible[None], jnp.exp(scores - log_total[:, :, None]), 0.0)
        share_grad = jnp.einsum(
            "qhd,khd->hqk", grad_heads, value_block, preferred_element_type=jnp.float32
        )
        score_grad = (shares * (share_grad - delta[:, :, None])).astype(jnp.bfloat16)
        query_part = (
            jnp.einsum("hqk,khd->qhd", score_grad, key_block, preferred_element_type=jnp.float32)
            * 0.125
        )
        query_grad, key_grad, value_grad = carry
        value_part = jnp.einsum(
            "hqk,qhd->khd",
            shares.astype(jnp.bfloat16),
            grad_heads,
            preferred_element_type=jnp.float32,
        )
        key_part = (
            jnp.einsum("hqk,qhd->khd", score_grad, queries, preferred_element_type=jnp.float32)
            * 0.125
        )
        key_grad = lax.dynamic_update_slice_in_dim(key_grad, key_part, offset, 0)
        value_grad = lax.dynamic_update_slice_in_dim(value_grad, value_part, offset, 0)
        return (query_grad + query_part, key_grad, value_grad)

    initial = (
        jnp.zeros((count, heads, head_size), jnp.float32),
        jnp.zeros((group, heads, head_size), jnp.float32),
        jnp.zeros((group, heads, head_size), jnp.float32),
    )
    return lax.fori_loop(lower, upper, visit, initial)


def adamw(weight, gradient, first, second, rate, factor):
    clipped = gradient * factor
    first_new = BETA_FIRST * first + (1.0 - BETA_FIRST) * clipped
    second_new = BETA_SECOND * second + (1.0 - BETA_SECOND) * clipped * clipped
    corrected_first = first_new / (1.0 - BETA_FIRST**STEP)
    corrected_second = second_new / (1.0 - BETA_SECOND**STEP)
    weight_new = weight - rate * (
        corrected_first / (jnp.sqrt(corrected_second) + ADAM_EPSILON) + DECAY * weight
    )
    return (first_new, second_new, weight_new)


def per_device(
    inputs,
    cotangent,
    target_slot,
    anchor_slot,
    sequence_start,
    attention_in,
    attention_out,
    gate_up,
    feed_down,
    norm_gains,
    first_in,
    first_out,
    first_gate,
    first_down,
    first_gains,
    second_in,
    second_out,
    second_gate,
    second_down,
    second_gains,
):
    owners = lax.axis_size("dp")
    spans = lax.axis_size("seq")
    rows, width = inputs.shape
    per_owner = rows // owners
    capacity = per_owner + per_owner // 2
    slots = owners * capacity
    group = rows * spans
    heads = width // HEAD
    first_row = lax.axis_index("seq") * rows

    def to_slots(values, index):
        filled = jnp.zeros((slots, values.shape[1]), values.dtype).at[index].set(values)
        return filled.reshape(owners, capacity, values.shape[1])

    arrived_in, arrived_upstream = (
        lax.all_to_all(
            to_slots(inputs, target_slot), "dp", split_axis=0, concat_axis=0, tiled=True
        ),
        lax.all_to_all(
            to_slots(cotangent, target_slot), "dp", split_axis=0, concat_axis=0, tiled=True
        ),
    )
    balanced_in = jnp.take(arrived_in.reshape(slots, width), anchor_slot, axis=0)
    upstream = jnp.take(arrived_upstream.reshape(slots, width), anchor_slot, axis=0)
    weight_in, weight_out, weight_gate, weight_down, gain_rows = (
        lax.all_gather(attention_in.astype(jnp.bfloat16), ("dp", "seq"), axis=0, tiled=True),
        lax.all_gather(attention_out.astype(jnp.bfloat16), ("dp", "seq"), axis=0, tiled=True),
        lax.all_gather(gate_up.astype(jnp.bfloat16), ("dp", "seq"), axis=0, tiled=True),
        lax.all_gather(feed_down.astype(jnp.bfloat16), ("dp", "seq"), axis=0, tiled=True),
        lax.all_gather(norm_gains.astype(jnp.bfloat16), ("dp", "seq"), axis=1, tiled=True),
    )
    gain_rows = gain_rows.astype(jnp.float32)
    residual = balanced_in.astype(jnp.float32)
    normed_one, normal_one, inverse_one = norm_rows(residual, gain_rows[0])
    normed_one = normed_one.astype(jnp.bfloat16)
    mixed = jnp.dot(normed_one, weight_in, preferred_element_type=jnp.float32)
    positions = (first_row + jnp.arange(rows, dtype=jnp.int32) - sequence_start).astype(jnp.float32)
    cosine_table, sine_table = rope_tables(positions, HEAD)
    queries = rotate(mixed[:, :width].reshape(rows, heads, HEAD), cosine_table, sine_table).astype(
        jnp.bfloat16
    )
    key_local = rotate(
        mixed[:, width : 2 * width].reshape(rows, heads, HEAD), cosine_table, sine_table
    ).astype(jnp.bfloat16)
    value_local = mixed[:, 2 * width :].astype(jnp.bfloat16)
    key_rows, value_rows = (
        lax.all_gather(key_local.reshape(rows, width), "seq", axis=0, tiled=True),
        lax.all_gather(value_local, "seq", axis=0, tiled=True),
    )
    key_rows = key_rows.reshape(group, heads, HEAD)
    value_rows = value_rows.reshape(group, heads, HEAD)
    attended, log_total = attend(queries, key_rows, value_rows, sequence_start, first_row, BLOCK)
    attended_low = attended.reshape(rows, width).astype(jnp.bfloat16)
    middle = residual + jnp.dot(attended_low, weight_out, preferred_element_type=jnp.float32)
    normed_two, normal_two, inverse_two = norm_rows(middle, gain_rows[1])
    normed_two = normed_two.astype(jnp.bfloat16)
    gate_values = jnp.dot(normed_two, weight_gate, preferred_element_type=jnp.float32)
    hidden_width = weight_down.shape[0]
    gate_part = gate_values[:, :hidden_width]
    up_part = gate_values[:, hidden_width:]
    sigmoid_gate = jax.nn.sigmoid(gate_part)
    activated = gate_part * sigmoid_gate
    hidden = (activated * up_part).astype(jnp.bfloat16)
    result = middle + jnp.dot(hidden, weight_down, preferred_element_type=jnp.float32)
    result_low = result.astype(jnp.bfloat16)
    down_grad = jnp.dot(hidden.T, upstream, preferred_element_type=jnp.float32)
    hidden_grad = jnp.dot(upstream, weight_down.T, preferred_element_type=jnp.float32)
    gate_grad = hidden_grad * up_part * sigmoid_gate * (1.0 + gate_part * (1.0 - sigmoid_gate))
    up_grad = hidden_grad * activated
    mixed_two_grad = jnp.concatenate([gate_grad, up_grad], axis=1).astype(jnp.bfloat16)
    gate_weight_grad = jnp.dot(normed_two.T, mixed_two_grad, preferred_element_type=jnp.float32)
    normed_two_grad = jnp.dot(mixed_two_grad, weight_gate.T, preferred_element_type=jnp.float32)
    middle_norm_grad, gain_two_grad = norm_back(
        normed_two_grad, normal_two, inverse_two, gain_rows[1]
    )
    middle_grad = upstream.astype(jnp.float32) + middle_norm_grad
    branch_grad = middle_grad.astype(jnp.bfloat16)
    out_weight_grad = jnp.dot(attended_low.T, branch_grad, preferred_element_type=jnp.float32)
    grad_heads = (
        jnp.dot(branch_grad, weight_out.T, preferred_element_type=jnp.float32)
        .astype(jnp.bfloat16)
        .reshape(rows, heads, HEAD)
    )
    delta = jnp.einsum("qhd,qhd->hq", grad_heads.astype(jnp.float32), attended)
    query_grad, key_grad, value_grad = attend_back(
        queries,
        key_rows,
        value_rows,
        sequence_start,
        first_row,
        BLOCK,
        grad_heads,
        log_total,
        delta,
    )
    key_own, value_own = (
        lax.psum_scatter(
            key_grad.reshape(group, width).astype(jnp.bfloat16),
            "seq",
            scatter_dimension=0,
            tiled=True,
        ).astype(jnp.float32),
        lax.psum_scatter(
            value_grad.reshape(group, width).astype(jnp.bfloat16),
            "seq",
            scatter_dimension=0,
            tiled=True,
        ).astype(jnp.float32),
    )
    query_pre = rotate_back(query_grad, cosine_table, sine_table).reshape(rows, width)
    key_pre = rotate_back(key_own.reshape(rows, heads, HEAD), cosine_table, sine_table).reshape(
        rows, width
    )
    mixed_grad = jnp.concatenate([query_pre, key_pre, value_own], axis=1).astype(jnp.bfloat16)
    in_weight_grad = jnp.dot(normed_one.T, mixed_grad, preferred_element_type=jnp.float32)
    normed_one_grad = jnp.dot(mixed_grad, weight_in.T, preferred_element_type=jnp.float32)
    residual_norm_grad, gain_one_grad = norm_back(
        normed_one_grad, normal_one, inverse_one, gain_rows[0]
    )
    input_low = (middle_grad + residual_norm_grad).astype(jnp.bfloat16)
    returned_out, returned_grad = (
        lax.all_to_all(
            to_slots(result_low, anchor_slot), "dp", split_axis=0, concat_axis=0, tiled=True
        ),
        lax.all_to_all(
            to_slots(input_low, anchor_slot), "dp", split_axis=0, concat_axis=0, tiled=True
        ),
    )
    outputs = jnp.take(returned_out.reshape(slots, width), target_slot, axis=0)
    input_gradient = jnp.take(returned_grad.reshape(slots, width), target_slot, axis=0)
    in_shard, out_shard, gate_shard, down_shard, gain_shard = (
        lax.psum_scatter(in_weight_grad, ("dp", "seq"), scatter_dimension=0, tiled=True),
        lax.psum_scatter(out_weight_grad, ("dp", "seq"), scatter_dimension=0, tiled=True),
        lax.psum_scatter(gate_weight_grad, ("dp", "seq"), scatter_dimension=0, tiled=True),
        lax.psum_scatter(down_grad, ("dp", "seq"), scatter_dimension=0, tiled=True),
        lax.psum_scatter(
            jnp.stack([gain_one_grad, gain_two_grad]),
            ("dp", "seq"),
            scatter_dimension=1,
            tiled=True,
        ),
    )
    local_total = (
        jnp.sum(in_shard * in_shard)
        + jnp.sum(out_shard * out_shard)
        + jnp.sum(gate_shard * gate_shard)
        + jnp.sum(down_shard * down_shard)
        + jnp.sum(gain_shard * gain_shard)
    )
    total = lax.psum(local_total, ("dp", "seq"))
    gradient_norm = jnp.sqrt(total)
    factor = CLIP / jnp.maximum(gradient_norm, CLIP)
    first_a, second_a, weight_a = adamw(
        attention_in, in_shard, first_in, second_in, D ** (-0.5), factor
    )
    first_b, second_b, weight_b = adamw(
        attention_out, out_shard, first_out, second_out, 0.5, factor
    )
    first_c, second_c, weight_c = adamw(
        gate_up, gate_shard, first_gate, second_gate, D ** (-0.5), factor
    )
    first_d, second_d, weight_d = adamw(
        feed_down, down_shard, first_down, second_down, 2.0 * FF ** (-0.5), factor
    )
    first_e, second_e, weight_e = adamw(
        norm_gains, gain_shard, first_gains, second_gains, 1.5, factor
    )
    return (
        outputs,
        input_gradient,
        gradient_norm,
        first_a,
        second_a,
        weight_a,
        first_b,
        second_b,
        weight_b,
        first_c,
        second_c,
        weight_c,
        first_d,
        second_d,
        weight_d,
        first_e,
        second_e,
        weight_e,
    )


def solution(mesh):
    in_specs = (
        P(("dp", "seq"), None),
        P(("dp", "seq"), None),
        P(("dp", "seq")),
        P(("dp", "seq")),
        P(("dp", "seq")),
        P(("dp", "seq"), None),
        P(("dp", "seq"), None),
        P(("dp", "seq"), None),
        P(("dp", "seq"), None),
        P(None, ("dp", "seq")),
        P(("dp", "seq"), None),
        P(("dp", "seq"), None),
        P(("dp", "seq"), None),
        P(("dp", "seq"), None),
        P(None, ("dp", "seq")),
        P(("dp", "seq"), None),
        P(("dp", "seq"), None),
        P(("dp", "seq"), None),
        P(("dp", "seq"), None),
        P(None, ("dp", "seq")),
    )
    out_specs = (
        P(("dp", "seq"), None),
        P(("dp", "seq"), None),
        P(),
        P(("dp", "seq"), None),
        P(("dp", "seq"), None),
        P(("dp", "seq"), None),
        P(("dp", "seq"), None),
        P(("dp", "seq"), None),
        P(("dp", "seq"), None),
        P(("dp", "seq"), None),
        P(("dp", "seq"), None),
        P(("dp", "seq"), None),
        P(("dp", "seq"), None),
        P(("dp", "seq"), None),
        P(("dp", "seq"), None),
        P(None, ("dp", "seq")),
        P(None, ("dp", "seq")),
        P(None, ("dp", "seq")),
    )
    return jax.shard_map(
        per_device, mesh=mesh, in_specs=in_specs, out_specs=out_specs, check_vma=False
    )
```

profile of v0, /device:TPU:0, one launch (start us, length us, event | category | flops | bytes accessed | tf_op | source)
XLA Modules:
  0.0 2086.6 jit_solution(7141028846655005243)
XLA Ops:
  19.4 69.0 %all-gather = bf16[32,32,2]{1,2,0:T(2,128)(2,1)S(1)} all-gather(bf16[1,32,2]{1,2,0:T(2,128)(2,1)S(1)} %convert_bitcast_fusion), channel_id=1, replica_groups=mesh['dp'=8,'seq'=4] {'dp','seq'}, dimensions={0}, use_global_device_ids=true | all-gather | bytes 4224 | tf_op jit(solution)/shard_map/all_gather | solution.py:217
  131.0 16.7 all-to-all-done.2
  153.3 24.6 %all-gather.12.cloned.1.call-done = bf16[2048,1024]{1,0:T(8,128)(2,1)} async-done(((bf16[512,1024]{1,0:T(8,128)(2,1)}), bf16[2048,1024]{1,0:T(8,128)(2,1)}) %all-gather.12.cloned.1.call-update) | async-done | bytes 4194320 | tf_op jit(solution)/shard_map/all_gather | solution.py:235
  184.4 75.0 %all-gather.10.cloned.1.call-done = bf16[2048,1024]{1,0:T(8,128)(2,1)} async-done(((bf16[512,1024]{1,0:T(8,128)(2,1)}), bf16[2048,1024]{1,0:T(8,128)(2,1)}) %all-gather.10.cloned.1.call-update) | async-done | bytes 4194320 | tf_op jit(solution)/shard_map/all_gather | solution.py:234
  266.3 14.2 while.30
  282.0 35.9 %all-gather.14.cloned.1.call-done = bf16[1024,1024]{1,0:T(8,128)(2,1)} async-done(((bf16[32,1024]{1,0:T(8,128)(2,1)}), bf16[1024,1024]{1,0:T(8,128)(2,1)}) %all-gather.14.cloned.1.call-update) | async-done | bytes 2097168 | tf_op jit(solution)/shard_map/all_gather | solution.py:214
  321.5 89.8 %all-gather.16.cloned.1.call-done = bf16[1024,5632]{1,0:T(8,128)(2,1)} async-done(((bf16[32,5632]{1,0:T(8,128)(2,1)}), bf16[1024,5632]{1,0:T(8,128)(2,1)}) %all-gather.16.cloned.1.call-update) | async-done | bytes 11534352 | tf_op jit(solution)/shard_map/all_gather | solution.py:215
  411.3 28.5 %fusion.94 = f32[512,5632]{1,0:T(8,128)} fusion(bf16[1024,5632]{1,0:T(8,128)(2,1)} %all-gather.16.cloned.1.call-done, f32[512,1024]{1,0:T(8,128)S(1)} %get-tuple-element.323, f32[1024]{0:T(1024)S(1)} %bitcast.173, f32[512]{0:T(512)S(1)} %add_rsqrt_fusion), kind=kOutput, calls=%fused_computation.178 | convolution fusion | flops 5907152896 | bytes 25171968 | tf_op jit(solution)/shard_map/dot_general | solution.py:244
  439.8 40.5 %all-gather.18.cloned.1.call-done = bf16[2816,1024]{1,0:T(8,128)(2,1)} async-done(((bf16[88,1024]{1,0:T(8,128)(2,1)}), bf16[2816,1024]{1,0:T(8,128)(2,1)}) %all-gather.18.cloned.1.call-update) | async-done | bytes 5767184 | tf_op jit(solution)/shard_map/all_gather | solution.py:216
  480.3 12.8 multiply_convert_fusion.1
  493.1 13.3 multiply_reduce_fusion
  521.9 38.9 %while.31 = (s32[]{:T(128)}, f32[512,16,64]{0,2,1:T(8,128)S(1)}, bf16[2048,16,64]{0,2,1:T(8,128)(2,1)}, bf16[2048,16,64]{0,2,1:T(8,128)(2,1)}, s32[]{:T(128)}, /...) while((s32[]{:T(128)}, f32[512,16,64]{0,2,1:T(8,128)S(1)}, ...), condition=%wide.region_11.13_spmd.clone, body=%wide.region_10.12_spmd.clone.sunk | while | flops 2737046528 | bytes 125675808 | solution.py:151
  531.6 11.4 bitcast_dynamic-update-slice_fusion.5
  543.0 10.0 fusion.160
  567.0 185.5 %reduce-scatter.10.cloned.1.call-done = bf16[512,1024]{0,1:T(8,128)(2,1)} async-done(((bf16[2048,1024]{0,1:T(8,128)(2,1)}), bf16[512,1024]{0,1:T(8,128)(2,1)}) %reduce-scatter.10.cloned.1.call-update) | async-done | bytes 1048592 | tf_op jit(solution)/shard_map/reduce_scatter | solution.py:284
  759.5 72.8 %reduce-scatter.12.cloned.1.call-done = bf16[512,1024]{0,1:T(8,128)(2,1)} async-done(((bf16[2048,1024]{0,1:T(8,128)(2,1)}), bf16[512,1024]{0,1:T(8,128)(2,1)}) %reduce-scatter.12.cloned.1.call-update) | async-done | bytes 1048592 | tf_op jit(solution)/shard_map/reduce_scatter | solution.py:290
  863.0 13.7 fusion.42
  899.0 17.8 all-to-all-done.1
  923.3 60.2 %reduce-scatter.16.cloned.1.call-done = f32[32,1024]{1,0:T(8,128)} async-done(((f32[1024,1024]{1,0:T(8,128)}), f32[32,1024]{1,0:T(8,128)}) %reduce-scatter.16.cloned.1.call-update) | async-done | bytes 131088 | tf_op jit(solution)/shard_map/reduce_scatter | solution.py:320
  985.0 134.6 %reduce-scatter.22.cloned.1.call-done = f32[32,2]{1,0:T(8,128)} async-done(((f32[1024,2]{1,0:T(8,128)}), f32[32,2]{1,0:T(8,128)}) %reduce-scatter.22.cloned.1.call-update) | async-done | bytes 272
  1123.8 245.3 %reduce-scatter.20.cloned.1.call-done = f32[88,1024]{1,0:T(8,128)} async-done(((f32[2816,1024]{1,0:T(8,128)}), f32[88,1024]{1,0:T(8,128)}) %reduce-scatter.20.cloned.1.call-update) | async-done | bytes 360464 | tf_op jit(solution)/shard_map/reduce_scatter | solution.py:322
  1370.8 158.5 %reduce-scatter.14.cloned.1.call-done = f32[32,3072]{1,0:T(8,128)} async-done(((f32[1024,3072]{1,0:T(8,128)}), f32[32,3072]{1,0:T(8,128)}) %reduce-scatter.14.cloned.1.call-update) | async-done | bytes 393232 | tf_op jit(solution)/shard_map/reduce_scatter | solution.py:319
  1532.3 492.8 %reduce-scatter.18.cloned.1.call-done = f32[32,5632]{1,0:T(8,128)} async-done(((f32[1024,5632]{1,0:T(8,128)}), f32[32,5632]{1,0:T(8,128)}) %reduce-scatter.18.cloned.1.call-update) | async-done | bytes 720912 | tf_op jit(solution)/shard_map/reduce_scatter | solution.py:321
  2032.0 38.7 %psum.7 = f32[]{:T(128)} all-reduce(f32[]{:T(128)S(6)} %add.255), channel_id=1, replica_groups=mesh['dp'=8,'seq'=4] {'dp','seq'}, use_global_device_ids=true, to_apply=%region_28.30 | all-reduce | flops 1 | bytes 8 | tf_op jit(solution)/shard_map/psum | solution.py:337
  (252 shorter events, 215.7 us)
Async XLA Ops:
  7.2 84.0 %all-gather.8.cloned.1.call-start = ((), (), s32[]{:S(2)}) async-start(), calls=%async_computation.11 | async-start | bytes 6488064 | tf_op jit(solution)/shard_map/all_gather | solution.py:213
  9.6 109.1 %copy-start.51 = (s32[512]{0:T(512)}, s32[512]{0:T(512)S(1)}, u32[]{:S(2)}) copy-start(s32[512]{0:T(512)S(1)} %compare_select_fusion) | copy-start | bytes 6148
  14.2 74.5 %all-to-all-start = ((bf16[8,96,1024]{2,1,0:T(8,128)(2,1)}), bf16[8,96,1024]{2,1,0:T(8,128)(2,1)S(1)}, u32[]{:S(2)}, u32[]{:S(2)}) async-start(bf16[8,96,1024]{2,1,0:T(8,128)(2,1)} %bitcast.2), calls=%async_computation | async-start | bytes 3145728 | tf_op jit(solution)/shard_map/all_to_all | solution.py:203
  19.3 158.6 %all-gather.12.cloned.1.call-start = ((), (), s32[]{:S(2)}) async-start(), calls=%async_computation.13 | async-start | bytes 5242880 | tf_op jit(solution)/shard_map/all_gather | solution.py:235
  88.6 417.9 %copy-start.45 = (pred[512]{0:T(512)(128)(4,1)}, pred[512]{0:T(512)(128)(4,1)S(1)}, u32[]{:S(2)}) copy-start(pred[512]{0:T(512)(128)(4,1)S(1)} %compare_and_fusion.3) | copy-start | bytes 1540
  88.6 417.8 %copy-start.36 = (f32[1,1024]{1,0:T(1,128)}, f32[1,1024]{1,0:T(1,128)S(1)}, u32[]{:S(2)}) copy-start(f32[1,1024]{1,0:T(1,128)S(1)} %get-tuple-element.315) | copy-start | bytes 12292
  100.9 158.5 %all-gather.10.cloned.1.call-start = ((), (), s32[]{:S(2)}) async-start(), calls=%async_computation.12 | async-start | bytes 5242880 | tf_op jit(solution)/shard_map/all_gather | solution.py:234
  117.1 200.8 %all-gather.14.cloned.1.call-start = ((), (), s32[]{:S(2)}) async-start(), calls=%async_computation.14 | async-start | bytes 2162688 | tf_op jit(solution)/shard_map/all_gather | solution.py:214
  117.8 293.4 %all-gather.16.cloned.1.call-start = ((), (), s32[]{:S(2)}) async-start(), calls=%async_computation.15 | async-start | bytes 11894784 | tf_op jit(solution)/shard_map/all_gather | solution.py:215
  123.2 24.5 %all-to-all-start.2 = ((bf16[8,96,1024]{2,1,0:T(8,128)(2,1)}), bf16[8,96,1024]{2,1,0:T(8,128)(2,1)S(1)}, u32[]{:S(2)}, u32[]{:S(2)}) async-start(bf16[8,96,1024]{2,1,0:T(8,128)(2,1)} %bitcast.20), calls=%async_computation.2 | async-start | bytes 3145728 | tf_op jit(solution)/shard_map/all_to_all | solution.py:206
  126.8 353.5 %all-gather.18.cloned.1.call-start = ((), (), s32[]{:S(2)}) async-start(), calls=%async_computation.16 | async-start | bytes 5947392 | tf_op jit(solution)/shard_map/all_gather | solution.py:216
  127.6 625.0 %reduce-scatter.10.cloned.1.call-start = ((), (), s32[]{:S(2)}) async-start(), calls=%async_computation.17 | async-start | bytes 5242880 | tf_op jit(solution)/shard_map/reduce_scatter | solution.py:284
  321.5 185.0 %copy-start = (f32[512,1024]{1,0:T(8,128)}, f32[512,1024]{1,0:T(8,128)S(1)}, u32[]{:S(2)}) copy-start(f32[512,1024]{1,0:T(8,128)S(1)} %get-tuple-element.323) | copy-start | bytes 6291460
  321.5 185.0 %copy-start.43 = (f32[512]{0:T(512)}, f32[512]{0:T(512)S(1)}, u32[]{:S(2)}) copy-start(f32[512]{0:T(512)S(1)} %add_rsqrt_fusion) | copy-start | bytes 6148
  560.9 271.4 %reduce-scatter.12.cloned.1.call-start = ((), (), s32[]{:S(2)}) async-start(), calls=%async_computation.18 | async-start | bytes 5242880 | tf_op jit(solution)/shard_map/reduce_scatter | solution.py:290
  561.6 421.8 %reduce-scatter.16.cloned.1.call-start = ((), (), s32[]{:S(2)}) async-start(), calls=%async_computation.20 | async-start | bytes 4325376 | tf_op jit(solution)/shard_map/reduce_scatter | solution.py:320
  567.0 185.6 %copy-start.22 = (f32[512,64]{0,1:T(8,128)S(1)}, f32[512,64]{0,1:T(8,128)}, u32[]{:S(2)}) copy-start(f32[512,64]{0,1:T(8,128)} %copy-done.21) | copy-start | bytes 393220
  567.0 552.6 %reduce-scatter.22.cloned.1.call-start = ((), (), s32[]{:S(2)}) async-start(), calls=%async_computation.23 | async-start | bytes 540672
  842.3 526.8 %reduce-scatter.20.cloned.1.call-start = ((), (), s32[]{:S(2)}) async-start(), calls=%async_computation.22 | async-start | bytes 11894784 | tf_op jit(solution)/shard_map/reduce_scatter | solution.py:322
  850.3 679.0 %reduce-scatter.14.cloned.1.call-start = ((), (), s32[]{:S(2)}) async-start(), calls=%async_computation.19 | async-start | bytes 12976128 | tf_op jit(solution)/shard_map/reduce_scatter | solution.py:319
  861.4 1163.7 %reduce-scatter.18.cloned.1.call-start = ((), (), s32[]{:S(2)}) async-start(), calls=%async_computation.21 | async-start | bytes 23789568 | tf_op jit(solution)/shard_map/reduce_scatter | solution.py:321
  889.0 27.8 %all-to-all-start.1 = ((bf16[8,96,1024]{2,1,0:T(8,128)(2,1)}), bf16[8,96,1024]{2,1,0:T(8,128)(2,1)S(1)}, u32[]{:S(2)}, u32[]{:S(2)}) async-start(bf16[8,96,1024]{2,1,0:T(8,128)(2,1)} %bitcast.163), calls=%async_computation.1 | async-start | bytes 3145728 | tf_op jit(solution)/shard_map/all_to_all | solution.py:309
  916.8 204.2 %all-to-all-start.3 = ((bf16[8,96,1024]{2,1,0:T(8,128)(2,1)}), bf16[8,96,1024]{2,1,0:T(8,128)(2,1)S(1)}, u32[]{:S(2)}, u32[]{:S(2)}) async-start(bf16[8,96,1024]{2,1,0:T(8,128)(2,1)} %bitcast.164), calls=%async_computation.5 | async-start | bytes 3145728 | tf_op jit(solution)/shard_map/all_to_all | solution.py:312
  1123.8 905.2 %copy-start.12 = (bf16[512,1024]{1,0:T(8,128)(2,1)S(1)}, bf16[512,1024]{1,0:T(8,128)(2,1)}, u32[]{:S(2)}) copy-start(bf16[512,1024]{1,0:T(8,128)(2,1)} %gather_fusion.1) | copy-start | bytes 3145732
  (54 other events, 1214.7 us)
Sparse Core Ops, SparseCore 0:
  11.5 74.9 all-gather.7
  101.0 76.8 all-gather.11
  180.1 79.2 all-gather.9
  262.8 55.0 all-gather.13
  321.1 90.1 all-gather.15
  414.6 65.6 all-gather.17
  561.0 191.5 reduce-scatter.9
  755.0 77.2 reduce-scatter.11
  834.5 148.8 reduce-scatter.15
  986.1 133.4 reduce-scatter.21
  1122.0 247.0 reduce-scatter.19
  1376.0 153.2 reduce-scatter.13
  1531.6 493.4 reduce-scatter.17
where the time goes:
time: 2100 us; the launch traced here: 2090 us
  waiting for transfers between devices  1650 us (79%)
  matrix products  165 us (8%)
  blocking collectives  108 us (5%)
  local copies, waits for them, and re-layouts  71.5 us (3%)
  other arithmetic  50.9 us (2%)
  between operations  22.7 us (1%)
    reduce_scatter x1, waiting for transfers between devices, per_device(): lax.psum_scatter(gate_weight_grad, ('dp', 'seq'), scatter_dimension=0, ti...  493 us
    reduce_scatter x1, waiting for transfers between devices, per_device(): lax.psum_scatter(down_grad, ('dp', 'seq'), scatter_dimension=0, tiled=True)  245 us
    reduce_scatter x1, waiting for transfers between devices, per_device(): lax.psum_scatter(key_grad.reshape(group, width).astype(jnp.bfloat16), 'se...  186 us
    reduce_scatter x1, waiting for transfers between devices, per_device(): lax.psum_scatter(in_weight_grad, ('dp', 'seq'), scatter_dimension=0, tile...  159 us
    unnamed x14, waiting for transfers between devices  135 us
    all_gather x1, waiting for transfers between devices, per_device(): lax.all_gather(gate_up.astype(jnp.bfloat16), ('dp', 'seq'), axis=0, tiled...  89.8 us
    all_gather x1, waiting for transfers between devices, per_device(): lax.all_gather(key_local.reshape(rows, width), 'seq', axis=0, tiled=True)  75 us
    reduce_scatter x1, waiting for transfers between devices, per_device(): lax.psum_scatter(value_grad.reshape(group, width).astype(jnp.bfloat16), '...  72.8 us
  transfers between devices with their start and end apart: 17, of which 14 were waited for; matrix products, arithmetic and copies ran while one was open for 9% of the time, Pallas kernels for 0%

commit v1 on v0

v1 whole, which is shorter than its diff:
```python
import functools

import jax
import jax.numpy as jnp
from jax import lax
from jax.experimental import pallas as pl
from jax.experimental.pallas import tpu as pltpu
from jax.sharding import Mesh
from jax.sharding import PartitionSpec as P

D = 1024
HEAD = 64
FF = 2816
STEP = 10
LANES = 128
TILE = 512

EPSILON = 1e-05
THETA = 500000.0
NEGATIVE = -1e30
BETA_FIRST = 0.9
BETA_SECOND = 0.95
ADAM_EPSILON = 1e-08
DECAY = 0.1
CLIP = 1.0
SCALE = 0.125
VMEM = 56 * 1024 * 1024
F32 = jnp.float32
BF16 = jnp.bfloat16
ROWS = ("chip", "core", "seq")


def norm_rows(values, gain_row):
    inverse = lax.rsqrt(jnp.mean(values * values, axis=1, keepdims=True) + EPSILON)
    normal = values * inverse
    return (normal * gain_row[None, :], normal, inverse)


def norm_back(upstream, normal, inverse, gain_row):
    gain_grad = jnp.sum(upstream * normal, axis=0)
    scaled = upstream * gain_row[None, :]
    return (
        inverse * (scaled - normal * jnp.mean(scaled * normal, axis=1, keepdims=True)),
        gain_grad,
    )


def rope_tables(positions):
    half_size = HEAD // 2
    frequency = jnp.power(THETA, -2.0 * jnp.arange(half_size, dtype=F32) / HEAD)
    angles = positions[:, None] * frequency[None, :]
    cosine = jnp.cos(angles)
    sine = jnp.sin(angles)
    return (
        jnp.concatenate([cosine] * 4, axis=1),
        jnp.concatenate([-sine, sine, -sine, sine], axis=1),
    )


def swap_halves(values):
    lane = lax.broadcasted_iota(jnp.int32, values.shape, 1)
    left = pltpu.roll(values, LANES - HEAD // 2, 1)
    right = pltpu.roll(values, HEAD // 2, 1)
    return jnp.where(lane % HEAD < HEAD // 2, left, right)


def contract_last(left, right):
    return lax.dot_general(left, right, (((1,), (1,)), ((), ())), preferred_element_type=F32)


def project_kernel(heads_width, spans, x_ref, gain_ref, w_ref, cos_ref, sin_ref, out_ref, h_ref):
    step = pl.program_id(0)

    @pl.when(step == 0)
    def _():
        x = x_ref[...].astype(F32)
        inverse = lax.rsqrt(jnp.mean(x * x, axis=1, keepdims=True) + EPSILON)
        h_ref[...] = (x * inverse * gain_ref[...]).astype(BF16)

    acc = jnp.dot(h_ref[...], w_ref[...], preferred_element_type=F32)

    @pl.when(step < 2 * spans)
    def _():
        for c in range(heads_width // LANES):
            part = acc[:, c * LANES : (c + 1) * LANES]
            turned = part * cos_ref[...] + swap_halves(part) * sin_ref[...]
            out_ref[0, :, c * LANES : (c + 1) * LANES] = turned.astype(BF16)

    @pl.when(step >= 2 * spans)
    def _():
        out_ref[0] = acc.astype(BF16)


def project(x, gain_row, weight, cosine, sine, spans):
    rows, width = x.shape
    hw = width // spans
    return pl.pallas_call(
        functools.partial(project_kernel, hw, spans),
        grid=(3 * spans,),
        in_specs=[
            pl.BlockSpec((rows, width), lambda t: (0, 0)),
            pl.BlockSpec((1, width), lambda t: (0, 0)),
            pl.BlockSpec((width, hw), lambda t: (0, t)),
            pl.BlockSpec((rows, LANES), lambda t: (0, 0)),
            pl.BlockSpec((rows, LANES), lambda t: (0, 0)),
        ],
        out_specs=[
            pl.BlockSpec((1, rows, hw), lambda t: (t % spans, 0, t // spans)),
            pl.BlockSpec((rows, width), lambda t: (0, 0)),
        ],
        out_shape=[
            jax.ShapeDtypeStruct((spans, rows, 3 * hw), BF16),
            jax.ShapeDtypeStruct((rows, width), BF16),
        ],
        compiler_params=pltpu.CompilerParams(vmem_limit_bytes=VMEM),
        cost_estimate=pl.CostEstimate(
            flops=2 * rows * width * 3 * width, bytes_accessed=12 * width * width, transcendentals=0
        ),
        name="project",
    )(x, gain_row, weight, cosine, sine)


def attend_kernel(block, start_ref, q_ref, k_ref, v_ref, low_ref, out_ref, log_ref):
    i = pl.program_id(1)
    lane = lax.broadcasted_iota(jnp.int32, (block, LANES), 1)
    first = lane < HEAD
    q_pair = q_ref[...] * SCALE
    query = i * block + lax.broadcasted_iota(jnp.int32, (block, block), 0)
    key = lax.broadcasted_iota(jnp.int32, (block, block), 1)
    starts = start_ref[...]
    parts = []
    for head in range(2):
        mine = first if head == 0 else jnp.logical_not(first)
        q = jnp.where(mine, q_pair, jnp.zeros_like(q_pair))

        def scores(j, diagonal, q=q):
            k = k_ref[pl.ds(pl.multiple_of(j * block, block), block), :]
            s = contract_last(q, k)
            seen = key + j * block >= starts
            if diagonal:
                seen = seen & (key + j * block <= query)
            return jnp.where(seen, s, NEGATIVE)

        def weigh(j, p):
            v = v_ref[pl.ds(pl.multiple_of(j * block, block), block), :]
            return jnp.dot(p.astype(BF16), v, preferred_element_type=F32)

        s = scores(i, True)
        top = jnp.max(s, axis=1, keepdims=True)
        p = jnp.exp(s - top)
        carry = (top, jnp.sum(p, axis=1, keepdims=True), weigh(i, p))

        def visit(j, carry):
            top, total, acc = carry
            s = scores(j, False)
            new = jnp.maximum(top, jnp.max(s, axis=1, keepdims=True))
            factor = jnp.exp(top - new)
            p = jnp.exp(s - new)
            return (
                new,
                total * factor + jnp.sum(p, axis=1, keepdims=True),
                acc * factor + weigh(j, p),
            )

        top, total, acc = lax.fori_loop(0, i, visit, carry)
        parts.append((acc / total, top + jnp.log(total)))
    out = jnp.where(first, parts[0][0], parts[1][0])
    out_ref[...] = out
    low_ref[...] = out.astype(BF16)
    logs = jnp.where(first, parts[0][1], parts[1][1]).T
    log_ref[0, 0:1, :] = logs[0:1]
    log_ref[0, 1:2, :] = logs[HEAD : HEAD + 1]


def attend(qkv, starts):
    group, width = qkv.shape
    hw = width // 3
    pairs = hw // LANES
    block = TILE
    return pl.pallas_call(
        functools.partial(attend_kernel, block),
        grid=(pairs, group // block),
        in_specs=[
            pl.BlockSpec((block, 1), lambda p, i: (i, 0)),
            pl.BlockSpec((block, LANES), lambda p, i: (i, p)),
            pl.BlockSpec((group, LANES), lambda p, i: (0, pairs + p)),
            pl.BlockSpec((group, LANES), lambda p, i: (0, 2 * pairs + p)),
        ],
        out_specs=[
            pl.BlockSpec((block, LANES), lambda p, i: (i, p)),
            pl.BlockSpec((block, LANES), lambda p, i: (i, p)),
            pl.BlockSpec((1, 8, block), lambda p, i: (p, 0, i)),
        ],
        out_shape=[
            jax.ShapeDtypeStruct((group, hw), BF16),
            jax.ShapeDtypeStruct((group, hw), F32),
            jax.ShapeDtypeStruct((pairs, 8, group), F32),
        ],
        compiler_params=pltpu.CompilerParams(vmem_limit_bytes=VMEM),
        cost_estimate=pl.CostEstimate(
            flops=4 * group * group * hw, bytes_accessed=8 * group * width, transcendentals=0
        ),
        name="attend",
    )(starts.reshape(group, 1), qkv, qkv, qkv)


def attend_back_kernel(
    block,
    start_ref,
    q_ref,
    k_ref,
    v_ref,
    do_ref,
    out_ref,
    log_ref,
    cos_ref,
    sin_ref,
    dq_ref,
    dk_ref,
    dv_ref,
    delta_ref,
    turned_ref,
):
    j = pl.program_id(1)
    blocks = pl.num_programs(1)
    lane = lax.broadcasted_iota(jnp.int32, (block, LANES), 1)
    first = lane < HEAD

    @pl.when(j == 0)
    def _():
        def prepare(i, carry):
            at = pl.ds(pl.multiple_of(i * block, block), block)
            product = (do_ref[at, :].astype(F32) * out_ref[at, :]).T
            delta_ref[0:1, at] = jnp.sum(product[:HEAD], axis=0, keepdims=True)
            delta_ref[1:2, at] = jnp.sum(product[HEAD:], axis=0, keepdims=True)
            return carry

        lax.fori_loop(0, blocks, prepare, 0)
        turned_ref[...] = jnp.zeros_like(turned_ref)

    here = pl.ds(pl.multiple_of(j * block, block), block)
    k_pair = k_ref[here, :]
    v_pair = v_ref[here, :]
    k_turned = k_pair.astype(F32).T.astype(BF16)
    key = j * block + lax.broadcasted_iota(jnp.int32, (block, block), 0)
    query = lax.broadcasted_iota(jnp.int32, (block, block), 1)

    def visit(i, carry, diagonal):
        dk, dv = carry
        at = pl.ds(pl.multiple_of(i * block, block), block)
        q_pair = q_ref[at, :] * SCALE
        do_pair = do_ref[at, :]
        seen = key >= start_ref[:, at]
        if diagonal:
            seen = seen & (key <= query + i * block)
        for head in range(2):
            mine = first if head == 0 else jnp.logical_not(first)
            q = jnp.where(mine, q_pair, jnp.zeros_like(q_pair))
            do = jnp.where(mine, do_pair, jnp.zeros_like(do_pair))
            s = jnp.where(seen, contract_last(k_pair, q), NEGATIVE)
            p = jnp.exp(s - log_ref[0, head : head + 1, at])
            dp = contract_last(v_pair, do)
            ds = (p * (dp - delta_ref[head : head + 1, at])).astype(BF16)
            dv = dv + jnp.dot(p.astype(BF16), do, preferred_element_type=F32)
            dk = dk + jnp.dot(ds, q, preferred_element_type=F32)
            lines = slice(head * HEAD, (head + 1) * HEAD)
            turned_ref[lines, at] += jnp.dot(k_turned[lines], ds, preferred_element_type=F32)
        return (dk, dv)

    zero = jnp.zeros((block, LANES), F32)
    carry = visit(j, (zero, zero), True)
    dk, dv = lax.fori_loop(j + 1, blocks, lambda i, c: visit(i, c, False), carry)

    def turn_back(values, at):
        return values * cos_ref[at, :] + swap_halves(values * sin_ref[at, :])

    dk_ref[0] = turn_back(dk, here).astype(BF16)
    dv_ref[0] = dv.astype(BF16)

    @pl.when(j == blocks - 1)
    def _():
        def finish(i, carry):
            at = pl.ds(pl.multiple_of(i * block, block), block)
            dq_ref[0, at, :] = turn_back(turned_ref[:, at].T * SCALE, at).astype(BF16)
            return carry

        lax.fori_loop(0, blocks, finish, 0)


def attend_back(qkv, starts, do, out, logs, cosine, sine):
    group, width = qkv.shape
    hw = width // 3
    pairs = hw // LANES
    block = TILE
    whole = lambda p, j: (0, 0)
    return pl.pallas_call(
        functools.partial(attend_back_kernel, block),
        grid=(pairs, group // block),
        in_specs=[
            pl.BlockSpec((1, group), whole),
            pl.BlockSpec((group, LANES), lambda p, j: (0, p)),
            pl.BlockSpec((group, LANES), lambda p, j: (0, pairs + p)),
            pl.BlockSpec((group, LANES), lambda p, j: (0, 2 * pairs + p)),
            pl.BlockSpec((group, LANES), lambda p, j: (0, p)),
            pl.BlockSpec((group, LANES), lambda p, j: (0, p)),
            pl.BlockSpec((1, 8, group), lambda p, j: (p, 0, 0)),
            pl.BlockSpec((group, LANES), whole),
            pl.BlockSpec((group, LANES), whole),
        ],
        out_specs=[
            pl.BlockSpec((1, group, LANES), lambda p, j: (0, 0, p)),
            pl.BlockSpec((1, block, LANES), lambda p, j: (0, j, p)),
            pl.BlockSpec((1, block, LANES), lambda p, j: (0, j, p)),
        ],
        out_shape=[jax.ShapeDtypeStruct((1, group, hw), BF16)] * 3,
        scratch_shapes=[pltpu.VMEM((8, group), F32), pltpu.VMEM((LANES, group), F32)],
        compiler_params=pltpu.CompilerParams(vmem_limit_bytes=VMEM),
        cost_estimate=pl.CostEstimate(
            flops=10 * group * group * hw, bytes_accessed=12 * group * width, transcendentals=0
        ),
        name="attend_back",
    )(starts.reshape(1, group), qkv, qkv, qkv, do, out, logs, cosine, sine)


def adamw(weight, gradient, first, second, rate, factor):
    clipped = gradient * factor
    first_new = BETA_FIRST * first + (1.0 - BETA_FIRST) * clipped
    second_new = BETA_SECOND * second + (1.0 - BETA_SECOND) * clipped * clipped
    corrected_first = first_new / (1.0 - BETA_FIRST**STEP)
    corrected_second = second_new / (1.0 - BETA_SECOND**STEP)
    weight_new = weight - rate * (
        corrected_first / (jnp.sqrt(corrected_second) + ADAM_EPSILON) + DECAY * weight
    )
    return (first_new, second_new, weight_new)


def swap_core(values):
    return lax.ppermute(values, "core", [(0, 1), (1, 0)])


def gather_weight(shard):
    chips = lax.axis_size("chip")
    width = shard.shape[1]
    mine = lax.all_gather(shard.astype(BF16), ("chip", "seq"), axis=0, tiled=True)
    other = swap_core(mine)
    mine = mine.reshape(chips, 1, -1, width)
    other = other.reshape(chips, 1, -1, width)
    own = lax.axis_index("core") == 0
    both = jnp.where(
        own,
        jnp.concatenate([mine, other], axis=1),
        jnp.concatenate([other, mine], axis=1),
    )
    return both.reshape(-1, width)


def scatter_sum(gradient):
    chips = lax.axis_size("chip")
    rows, width = gradient.shape
    parts = gradient.reshape(chips, 2, -1, width)
    own = lax.axis_index("core") == 0
    mine = jnp.where(own, parts[:, 0], parts[:, 1])
    other = jnp.where(own, parts[:, 1], parts[:, 0]).astype(BF16)
    both = (mine + swap_core(other).astype(F32)).astype(BF16).reshape(-1, width)
    line = lax.psum_scatter(both, "chip", scatter_dimension=0, tiled=True)
    return lax.psum_scatter(line, "seq", scatter_dimension=0, tiled=True).astype(F32)


def sum_everywhere(values):
    for axis in ROWS:
        count = lax.axis_size(axis)
        step = 1
        while step < count:
            values = values + lax.ppermute(values, axis, [(i, i ^ step) for i in range(count)])
            step *= 2
    return values


def place(index, values, slots):
    chosen = lax.broadcasted_iota(jnp.int32, (slots, index.shape[0]), 0) == index[None, :]
    return jnp.dot(chosen.astype(BF16), values, preferred_element_type=F32).astype(BF16)


def pick(index, values):
    slots = values.shape[0]
    chosen = lax.broadcasted_iota(jnp.int32, (index.shape[0], slots), 1) == index[:, None]
    return jnp.dot(chosen.astype(BF16), values, preferred_element_type=F32).astype(BF16)


def per_device(
    inputs,
    cotangent,
    target_slot,
    anchor_slot,
    sequence_start,
    attention_in,
    attention_out,
    gate_up,
    feed_down,
    norm_gains,
    first_in,
    first_out,
    first_gate,
    first_down,
    first_gains,
    second_in,
    second_out,
    second_gate,
    second_down,
    second_gains,
):
    owners = lax.axis_size("chip") * lax.axis_size("core")
    spans = lax.axis_size("seq")
    rows, width = inputs.shape
    per_owner = rows // owners
    capacity = per_owner + per_owner // 2
    slots = owners * capacity
    group = rows * spans
    hw = width // spans
    first_row = lax.axis_index("seq") * rows

    def exchange(values):
        return lax.all_to_all(values, ("chip", "core"), split_axis=0, concat_axis=0, tiled=True)

    def across(values):
        return lax.all_to_all(values, "seq", split_axis=0, concat_axis=0, tiled=True)

    balanced_in = pick(anchor_slot, exchange(place(target_slot, inputs, slots)))
    upstream = pick(anchor_slot, exchange(place(target_slot, cotangent, slots)))
    gain_rows = lax.all_gather(norm_gains.astype(BF16), ROWS, axis=1, tiled=True).astype(F32)
    starts = lax.all_gather(sequence_start, "seq", axis=0, tiled=True)
    weight_in = gather_weight(attention_in)
    weight_out = gather_weight(attention_out)
    weight_gate = gather_weight(gate_up)
    weight_down = gather_weight(feed_down)

    local = first_row + jnp.arange(rows, dtype=jnp.int32) - sequence_start
    cosine, sine = rope_tables(local.astype(F32))
    cosine_all, sine_all = rope_tables((jnp.arange(group, dtype=jnp.int32) - starts).astype(F32))

    residual = balanced_in.astype(F32)
    cut, normed_one = project(balanced_in, gain_rows[0:1], weight_in, cosine, sine, spans)
    qkv = across(cut).reshape(group, 3 * hw)
    attended_cut, attended, logs = attend(qkv, starts)

    def whole_rows(values):
        return jnp.transpose(across(values.reshape(spans, rows, hw)), (1, 0, 2)).reshape(rows, width)

    attended_low = whole_rows(attended_cut)
    middle = residual + jnp.dot(attended_low, weight_out, preferred_element_type=F32)
    normed_two, normal_two, inverse_two = norm_rows(middle, gain_rows[1])
    normed_two = normed_two.astype(BF16)
    gate_values = jnp.dot(normed_two, weight_gate, preferred_element_type=F32)
    hidden_width = weight_down.shape[0]
    gate_part = gate_values[:, :hidden_width]
    up_part = gate_values[:, hidden_width:]
    sigmoid_gate = jax.nn.sigmoid(gate_part)
    activated = gate_part * sigmoid_gate
    hidden = (activated * up_part).astype(BF16)
    result = middle + jnp.dot(hidden, weight_down, preferred_element_type=F32)
    result_low = result.astype(BF16)
    down_grad = jnp.dot(hidden.T, upstream, preferred_element_type=F32)
    hidden_grad = jnp.dot(upstream, weight_down.T, preferred_element_type=F32)
    gate_grad = hidden_grad * up_part * sigmoid_gate * (1.0 + gate_part * (1.0 - sigmoid_gate))
    up_grad = hidden_grad * activated
    mixed_two_grad = jnp.concatenate([gate_grad, up_grad], axis=1).astype(BF16)
    gate_weight_grad = jnp.dot(normed_two.T, mixed_two_grad, preferred_element_type=F32)
    normed_two_grad = jnp.dot(mixed_two_grad, weight_gate.T, preferred_element_type=F32)
    middle_norm_grad, gain_two_grad = norm_back(
        normed_two_grad, normal_two, inverse_two, gain_rows[1]
    )
    middle_grad = upstream.astype(F32) + middle_norm_grad
    branch_grad = middle_grad.astype(BF16)
    out_weight_grad = jnp.dot(attended_low.T, branch_grad, preferred_element_type=F32)
    grad_heads = jnp.dot(branch_grad, weight_out.T, preferred_element_type=F32).astype(BF16)
    grad_cut = across(jnp.transpose(grad_heads.reshape(rows, spans, hw), (1, 0, 2)))
    grads = attend_back(
        qkv, starts, grad_cut.reshape(group, hw), attended, logs, cosine_all, sine_all
    )
    mixed_grad = jnp.concatenate([whole_rows(grad) for grad in grads], axis=1)
    in_weight_grad = jnp.dot(normed_one.T, mixed_grad, preferred_element_type=F32)
    normed_one_grad = jnp.dot(mixed_grad, weight_in.T, preferred_element_type=F32)
    _, normal_one, inverse_one = norm_rows(residual, gain_rows[0])
    residual_norm_grad, gain_one_grad = norm_back(
        normed_one_grad, normal_one, inverse_one, gain_rows[0]
    )
    input_low = (middle_grad + residual_norm_grad).astype(BF16)
    outputs = pick(target_slot, exchange(place(anchor_slot, result_low, slots)))
    input_gradient = pick(target_slot, exchange(place(anchor_slot, input_low, slots)))

    down_shard = scatter_sum(down_grad)
    gate_shard = scatter_sum(gate_weight_grad)
    out_shard = scatter_sum(out_weight_grad)
    in_shard = scatter_sum(in_weight_grad)
    gains_total = sum_everywhere(jnp.stack([gain_one_grad, gain_two_grad]))
    columns = norm_gains.shape[1]
    device = (lax.axis_index("chip") * 2 + lax.axis_index("core")) * spans + lax.axis_index("seq")
    gain_shard = lax.dynamic_slice_in_dim(gains_total, device * columns, columns, 1)
    local_total = (
        jnp.sum(in_shard * in_shard)
        + jnp.sum(out_shard * out_shard)
        + jnp.sum(gate_shard * gate_shard)
        + jnp.sum(down_shard * down_shard)
        + jnp.sum(gain_shard * gain_shard)
    )
    total = sum_everywhere(jnp.broadcast_to(local_total, (8, LANES)))[0, 0]
    gradient_norm = jnp.sqrt(total)
    factor = CLIP / jnp.maximum(gradient_norm, CLIP)
    updates = []
    for weight, gradient, first, second, rate in (
        (attention_in, in_shard, first_in, second_in, D ** (-0.5)),
        (attention_out, out_shard, first_out, second_out, 0.5),
        (gate_up, gate_shard, first_gate, second_gate, D ** (-0.5)),
        (feed_down, down_shard, first_down, second_down, 2.0 * FF ** (-0.5)),
        (norm_gains, gain_shard, first_gains, second_gains, 1.5),
    ):
        updates.extend(adamw(weight, gradient, first, second, rate, factor))
    return (outputs, input_gradient, gradient_norm, *updates)


def solution(mesh):
    owners, spans = mesh.shape["dp"], mesh.shape["seq"]
    parts = Mesh(mesh.devices.reshape(owners // 2, 2, spans), ROWS)
    rows = P(ROWS, None)
    columns = P(None, ROWS)
    line = P(ROWS)
    in_specs = (rows, rows, line, line, line) + ((rows,) * 4 + (columns,)) * 3
    out_specs = (rows, rows, P()) + (rows,) * 12 + (columns,) * 3
    return jax.shard_map(
        per_device, mesh=parts, in_specs=in_specs, out_specs=out_specs, check_vma=False
    )
```

time: 2100 us -> 949 us (0.45)
  waiting for transfers between devices: 1650 us -> 462 us
  Pallas kernels: 0 us -> 92.3 us
  matrix products: 165 us -> 98.3 us
  other arithmetic: 50.9 us -> 111 us
  local copies, waits for them, and re-layouts: 71.5 us -> 22 us
  starting transfers between devices: 17.2 us -> 54.6 us
  blocking collectives: 108 us -> 79.1 us
    reduce_scatter x6 -> x8, waiting for transfers between devices: 1220 us -> 167 us  [the longest x4 97.9 us: scatter_sum(): line = lax.psum_scatter(both, 'chip', scatter_dimension=0, tiled=True)]
    unnamed x14 -> x12, waiting for transfers between devices: 135 us -> 1.33 us
    pallas_call x0 -> x3, Pallas kernels: none -> 92.3 us  [the longest x1 42.2 us: attend_back(): pl.pallas_call(functools.partial(attend_back_kernel, block), grid=(pairs,...]
    dot_general x19 -> x18, matrix products: 165 us -> 98.3 us  [the longest x4 16.8 us: place(): jnp.dot(chosen.astype(BF16), values, preferred_element_type=F32)]
    all_gather x6 -> x4, waiting for transfers between devices: 266 us -> 203 us  [gather_weight(): lax.all_gather(shard.astype(BF16), ('chip', 'seq'), axis=0, tiled=True)]
    convert_element_type x8 -> x15, other arithmetic: 5.92 us -> 57.5 us  [the longest x4 33.9 us: scatter_sum(): both = (mine + swap_core(other).astype(F32)).astype(BF16).reshape(-1, width)]
    all_to_all x4 -> x10, waiting for transfers between devices: 34.6 us -> 74.4 us  [the longest x6 74.4 us: across(): lax.all_to_all(values, 'seq', split_axis=0, concat_axis=0, tiled=True)]
    psum x1 -> x0, blocking collectives: 38.7 us -> none  [per_device(): total = lax.psum(local_total, ('dp', 'seq'))]
  transfers between devices with their start and end apart: 17 -> 40, of which waited for: 14 -> 23; matrix products, arithmetic and copies ran while one was open for 9% -> 17% of each run, Pallas kernels for 0% -> 5%
where the time goes in v1:
time: 949 us; the launch traced here: 940 us
  waiting for transfers between devices  462 us (49%)
  other arithmetic  111 us (12%)
  matrix products  98.3 us (10%)
  Pallas kernels  92.3 us (10%)
  blocking collectives  79.1 us (8%)
  starting transfers between devices  54.6 us (6%)
  local copies, waits for them, and re-layouts  22 us (2%)
  between operations  20.5 us (2%)
    all_gather x4, waiting for transfers between devices, gather_weight(): lax.all_gather(shard.astype(BF16), ('chip', 'seq'), axis=0, tiled=True)  203 us
    reduce_scatter x4, waiting for transfers between devices, scatter_sum(): line = lax.psum_scatter(both, 'chip', scatter_dimension=0, tiled=True)  97.9 us
    all_to_all x6, waiting for transfers between devices, across(): lax.all_to_all(values, 'seq', split_axis=0, concat_axis=0, tiled=True)  74.4 us
    reduce_scatter x4, waiting for transfers between devices, scatter_sum(): lax.psum_scatter(line, 'seq', scatter_dimension=0, tiled=True).astype(F32)  69.1 us
    all_gather x1, blocking collectives, per_device(): lax.all_gather(norm_gains.astype(BF16), ROWS, axis=1, tiled=True)  67.2 us
    pallas_call x1, Pallas kernels, attend_back(): pl.pallas_call(functools.partial(attend_back_kernel, block), grid=(pairs,...  42.2 us
    pallas_call x1, Pallas kernels, attend(): pl.pallas_call(functools.partial(attend_kernel, block), grid=(pairs, grou...  36.2 us
    convert_element_type x4, other arithmetic, scatter_sum(): both = (mine + swap_core(other).astype(F32)).astype(BF16).reshape(-1, width)  33.9 us
  transfers between devices with their start and end apart: 40, of which 23 were waited for; matrix products, arithmetic and copies ran while one was open for 17% of the time, Pallas kernels for 5%

profile of v1, /device:TPU:0, one launch (start us, length us, event | category | flops | bytes accessed | tf_op | source)
XLA Modules:
  0.0 939.7 jit_solution(10142101493319855140)
XLA Ops:
  11.0 71.2 %all-gather.7.cloned.1.call-done = bf16[512,3072]{1,0:T(8,128)(2,1)} async-done(((bf16[32,3072]{1,0:T(8,128)(2,1)}), bf16[512,3072]{1,0:T(8,128)(2,1)}) %all-gather.7.cloned.1.call-update) | async-done | bytes 3145744 | tf_op jit(solution)/shard_map/all_gather | solution.py:344
  89.6 67.2 %all-gather.1 = bf16[32,32,2]{1,2,0:T(2,128)(2,1)S(1)} all-gather(bf16[1,32,2]{1,2,0:T(2,128)(2,1)S(1)} %convert_bitcast_fusion), channel_id=1, replica_groups=mesh['chip'=4,'core'=2,'seq'=4] {'chip','core','seq'}, dimensions={0}, use_global_device_ids=true | all-gather | bytes 4224 | tf_op jit(solution)/shard_map/all_gather | solution.py:430
  170.7 13.9 %project.1 = (bf16[4,512,768]{2,1,0:T(8,128)(2,1)}, bf16[512,1024]{1,0:T(8,128)(2,1)}) custom-call(bf16[512,1024]{1,0:T(8,128)(2,1)} %get-tuple-element.70.x_ref, f32[1,1024]{1,0:T(1,128)} %get-tuple-element.62.gain_ref, bf16[1024,3072]{1,0:T(8,128)(2,1)} %bitcast.214, f32[512,128]{1,0:T(8,128)} %get-tuple-element.72.cos_ref, ...), custom_call_target="tpu_custom_call" | custom-call | flops 3221225472 | bytes 12582912 | tf_op jit(solution)/shard_map/project/pallas_call | solution.py:97
  190.3 94.0 %all-gather.13.cloned.1.call-done = bf16[1408,1024]{1,0:T(8,128)(2,1)} async-done(((bf16[88,1024]{1,0:T(8,128)(2,1)}), bf16[1408,1024]{1,0:T(8,128)(2,1)}) %all-gather.13.cloned.1.call-update) | async-done | bytes 2883600 | tf_op jit(solution)/shard_map/all_gather | solution.py:344
  290.1 11.9 %all-gather = s32[4,1,512]{2,1,0:T(1,128)S(1)} all-gather(s32[1,1,512]{2,1,0:T(1,128)S(1)} %bitcast.256), channel_id=1, replica_groups=mesh['chip'=4,'core'=2,'seq'=4] {'seq'}, dimensions={0}, use_global_device_ids=true | all-gather | bytes 10240 | tf_op jit(solution)/shard_map/all_gather | solution.py:431
  303.3 38.0 %all-gather.9.cloned.1.call-done = bf16[512,1024]{1,0:T(8,128)(2,1)} async-done(((bf16[32,1024]{1,0:T(8,128)(2,1)}), bf16[512,1024]{1,0:T(8,128)(2,1)}) %all-gather.9.cloned.1.call-update) | async-done | bytes 1048592 | tf_op jit(solution)/shard_map/all_gather | solution.py:344
  341.3 36.2 %attend.1 = (bf16[2048,256]{1,0:T(8,128)(2,1)}, f32[2048,256]{1,0:T(8,128)}, f32[2,8,2048]{2,1,0:T(8,128)}) custom-call(s32[2048,1]{1,0:T(8,128)} %copy.120.start_ref, bf16[2048,768]{1,0:T(8,128)(2,1)} %bitcast.14.q_ref.k_ref.v_ref, bf16[2048,768]{1,0:T(8,128)(2,1)} %bitcast.14.q_ref.k_ref.v_ref, bf16[2048,768]{1,0:T(8,128)(2,1)} %bitcast.14.q_ref.k_ref.v_ref), custom_call_target="tpu_custom_call" | custom-call | flops 4294967296 | bytes 12582912 | tf_op jit(solution)/shard_map/attend/pallas_call | solution.py:180
  394.6 15.5 %all-to-all-done.2 = bf16[4,512,256]{1,2,0:T(8,128)(2,1)S(1)} async-done(((bf16[4,512,256]{1,2,0:T(8,128)(2,1)}), bf16[4,512,256]{1,2,0:T(8,128)(2,1)S(1)}, u32[]{:S(2)}, u32[]{:S(2)}) %all-to-all-start.2) | async-done | bytes 1048608 | tf_op jit(solution)/shard_map/all_to_all | solution.py:426
  412.7 9.9 %maximum_select_fusion = bf16[4,2,128,5632]{3,2,1,0:T(8,128)(2,1)S(1)} fusion(bf16[4,1,128,5632]{3,2,1,0:T(8,128)(2,1)} %bitcast.23, bf16[4,1,128,5632]{3,2,1,0:T(8,128)(2,1)} %bitcast.221, pred[]{:T(512)S(6)} %eq.26), kind=kLoop, calls=%fused_computation | loop fusion | flops 17301504 | bytes 23068672 | tf_op jit(solution)/shard_map/jit(_where)/select_n | solution.py:349
  431.6 9.9 %multiply_convert_fusion.1 = (bf16[512,2816]{1,0:T(8,128)(2,1)S(1)}, bf16[512,2816]{1,0:T(8,128)(2,1)}, bf16[512,2816]{1,0:T(8,128)(2,1)}) fusion(f32[512,5632]{1,0:T(8,128)} %fusion.79, bf16[512,1024]{1,0:T(8,128)(2,1)S(1)} %copy-done.18, bf16[2816,1024]{1,0:T(8,128)(2,1)S(1)} %bitcast.220), kind=kOutput, calls=%fused_computation.21 | convolution fusion | flops 2974416896 | bytes 27000832 | tf_op jit(solution)/shard_map/dot_general | solution.py:463
  441.5 13.2 %multiply_reduce_fusion = (f32[1024]{0:T(1024)S(1)}, f32[512]{0:T(512)S(1)}, f32[512,1024]{1,0:T(8,128)}) fusion(f32[512,1024]{1,0:T(8,128)S(1)} %get-tuple-element.67, f32[512]{0:T(512)S(1)} %add_rsqrt_fusion.1, f32[1024]{0:T(1024)S(1)} %bitcast.241, bf16[1024,5632]{1,0:T(8,128)(2,1)} %bitcast.209, bf16[512,2816]{1,0:T(8,128)(2,1)} %get-tuple-element.56, ...), kind=kOutput, calls=%fused_computation.48 | convolution fusion | flops 5920258560 | bytes 21508096 | tf_op jit(solution)/shard_map/dot_general | solution.py:468
  474.3 16.0 %all-to-all-done.5 = bf16[4,512,256]{2,1,0:T(8,128)(2,1)} async-done(((bf16[4,512,256]{2,1,0:T(8,128)(2,1)}), bf16[4,512,256]{2,1,0:T(8,128)(2,1)}, u32[]{:S(2)}, u32[]{:S(2)}) %all-to-all-start.5) | async-done | bytes 1048608 | tf_op jit(solution)/shard_map/all_to_all | solution.py:426
  490.3 42.2 %attend_back.1 = (bf16[1,2048,256]{2,1,0:T(8,128)(2,1)}, bf16[1,2048,256]{2,1,0:T(8,128)(2,1)}, bf16[1,2048,256]{2,1,0:T(8,128)(2,1)}) custom-call(s32[1,2048]{1,0:T(1,128)} %bitcast.246, bf16[2048,768]{1,0:T(8,128)(2,1)} %bitcast.14.q_ref.k_ref.v_ref, bf16[2048,768]{1,0:T(8,128)(2,1)} %bitcast.14.q_ref.k_ref.v_ref, ...), custom_call_target="tpu_custom_call" | custom-call | flops 10737418240 | bytes 18874368 | tf_op jit(solution)/shard_map/attend_back/pallas_call | solution.py:296
  574.9 19.1 %all-to-all-done.7 = bf16[4,512,256]{1,2,0:T(8,128)(2,1)} async-done(((bf16[4,512,256]{1,2,0:T(8,128)(2,1)}), bf16[4,512,256]{1,2,0:T(8,128)(2,1)}, u32[]{:S(2)}, u32[]{:S(2)}) %all-to-all-start.7) | async-done | bytes 1048608 | tf_op jit(solution)/shard_map/all_to_all | solution.py:426
  606.6 16.2 %all-to-all-done.8 = bf16[4,512,256]{1,2,0:T(8,128)(2,1)S(1)} async-done(((bf16[4,512,256]{1,2,0:T(8,128)(2,1)}), bf16[4,512,256]{1,2,0:T(8,128)(2,1)S(1)}, u32[]{:S(2)}, u32[]{:S(2)}) %all-to-all-start.8) | async-done | bytes 1048608 | tf_op jit(solution)/shard_map/all_to_all | solution.py:426
  635.3 14.1 %fusion.11 = f32[1024,5632]{1,0:T(8,128)} fusion(bf16[512,2816]{1,0:T(8,128)(2,1)} %get-tuple-element.56, bf16[512,2816]{1,0:T(8,128)(2,1)} %copy-done.11, f32[512,1024]{1,0:T(8,128)S(1)} %copy-done.5, f32[1024]{0:T(1024)S(1)} %bitcast.243, f32[512]{0:T(512)S(1)} %add_rsqrt_fusion.1), kind=kOutput, calls=%fused_computation.25 | convolution fusion | flops 5918687232 | bytes 30939136 | tf_op jit(solution)/shard_map/dot_general | solution.py:467
  649.4 10.9 %fusion.6 = bf16[4,128,5632]{2,1,0:T(8,128)(2,1)} fusion(f32[4,2,128,5632]{3,2,1,0:T(8,128)} %bitcast.199, pred[]{:T(512)S(6)} %eq.26), kind=kLoop, calls=%fused_computation.12 | loop fusion | flops 2883584 | bytes 17301504 | tf_op jit(solution)/shard_map/convert_element_type | solution.py:363
  670.3 13.4 %fusion.2 = bf16[4,128,5632]{2,1,0:T(8,128)(2,1)} fusion(bf16[4,128,5632]{2,1,0:T(8,128)(2,1)} %collective-permute-done.6, f32[4,2,128,5632]{3,2,1,0:T(8,128)} %bitcast.200, pred[]{:T(512)S(6)} %eq.26), kind=kLoop, calls=%fused_computation.4 | loop fusion | flops 11534336 | bytes 34603008 | tf_op jit(solution)/shard_map/convert_element_type | solution.py:364
  685.3 25.7 %reduce-scatter.9.cloned.1.call-done = bf16[128,3072]{1,0:T(8,128)(2,1)} async-done(((bf16[512,3072]{1,0:T(8,128)(2,1)}), bf16[128,3072]{1,0:T(8,128)(2,1)}) %reduce-scatter.9.cloned.1.call-update) | async-done | bytes 786448 | tf_op jit(solution)/shard_map/reduce_scatter | solution.py:365
  711.0 9.2 convolution_convert_fusion.2
  724.8 72.2 %reduce-scatter.17.cloned.1.call-done = bf16[128,5632]{1,0:T(8,128)(2,1)} async-done(((bf16[512,5632]{1,0:T(8,128)(2,1)}), bf16[128,5632]{1,0:T(8,128)(2,1)}) %reduce-scatter.17.cloned.1.call-update) | async-done | bytes 1441808 | tf_op jit(solution)/shard_map/reduce_scatter | solution.py:365
  827.9 14.2 %reduce-scatter.23.cloned.1.call-done = bf16[88,1024]{1,0:T(8,128)(2,1)} async-done(((bf16[352,1024]{1,0:T(8,128)(2,1)}), bf16[88,1024]{1,0:T(8,128)(2,1)}) %reduce-scatter.23.cloned.1.call-update) | async-done | bytes 180240 | tf_op jit(solution)/shard_map/reduce_scatter | solution.py:366
  843.7 23.1 %reduce-scatter.11.cloned.1.call-done = bf16[32,3072]{1,0:T(8,128)(2,1)} async-done(((bf16[128,3072]{1,0:T(8,128)(2,1)}), bf16[32,3072]{1,0:T(8,128)(2,1)}) %reduce-scatter.11.cloned.1.call-update) | async-done | bytes 196624 | tf_op jit(solution)/shard_map/reduce_scatter | solution.py:366
  869.7 31.8 %reduce-scatter.19.cloned.1.call-done = bf16[32,5632]{1,0:T(8,128)(2,1)} async-done(((bf16[128,5632]{1,0:T(8,128)(2,1)}), bf16[32,5632]{1,0:T(8,128)(2,1)}) %reduce-scatter.19.cloned.1.call-update) | async-done | bytes 360464 | tf_op jit(solution)/shard_map/reduce_scatter | solution.py:366
  (240 shorter events, 230.5 us)
Async XLA Ops:
  7.2 75.0 %all-gather.7.cloned.1.call-start = ((), (), s32[]{:S(2)}) async-start(), calls=%async_computation.18 | async-start | bytes 3342336 | tf_op jit(solution)/shard_map/all_gather | solution.py:344
  9.0 180.5 %all-gather.11.cloned.1.call-start = ((), (), s32[]{:S(2)}) async-start(), calls=%async_computation.20 | async-start | bytes 6127616 | tf_op jit(solution)/shard_map/all_gather | solution.py:344
  82.2 80.1 %collective-permute-start = (bf16[512,3072]{1,0:T(8,128)(2,1)}, bf16[512,3072]{1,0:T(8,128)(2,1)}, u32[]{:S(2)}, u32[]{:S(2)}) collective-permute-start(bf16[512,3072]{1,0:T(8,128)(2,1)} %all-gather.7.cloned.1.call-done), channel_id=1, source_target_pairs={{0,4},{4,0},{1,5},{5,1},{2,6},{6,2},{3,7},{7,3},{8,12},{12,8},{9,1... | collective-permute-start | bytes 9437192 | tf_op jit(solution)/shard_map/ppermute | solution.py:338
  85.0 74.7 %all-to-all-start = ((bf16[8,96,1024]{2,1,0:T(8,128)(2,1)}), bf16[8,96,1024]{2,1,0:T(8,128)(2,1)S(1)}, u32[]{:S(2)}, u32[]{:S(2)}) async-start(bf16[8,96,1024]{2,1,0:T(8,128)(2,1)} %bitcast.229), calls=%async_computation | async-start | bytes 3145728 | tf_op jit(solution)/shard_map/all_to_all | solution.py:423
  88.8 195.5 %all-gather.13.cloned.1.call-start = ((), (), s32[]{:S(2)}) async-start(), calls=%async_computation.21 | async-start | bytes 3063808 | tf_op jit(solution)/shard_map/all_gather | solution.py:344
  184.6 101.8 %all-to-all-start.1 = ((bf16[4,512,768]{2,1,0:T(8,128)(2,1)}), bf16[4,512,768]{2,1,0:T(8,128)(2,1)}, u32[]{:S(2)}, u32[]{:S(2)}) async-start(bf16[4,512,768]{2,1,0:T(8,128)(2,1)} %get-tuple-element.26), calls=%async_computation.1 | async-start | bytes 6291456 | tf_op jit(solution)/shard_map/all_to_all | solution.py:426
  189.5 151.8 %all-gather.9.cloned.1.call-start = ((), (), s32[]{:S(2)}) async-start(), calls=%async_computation.19 | async-start | bytes 1114112 | tf_op jit(solution)/shard_map/all_gather | solution.py:344
  189.5 223.1 %collective-permute-start.2 = (bf16[512,5632]{1,0:T(8,128)(2,1)}, bf16[512,5632]{1,0:T(8,128)(2,1)}, u32[]{:S(2)}, u32[]{:S(2)}) collective-permute-start(bf16[512,5632]{1,0:T(8,128)(2,1)} %all-gather.11.cloned.1.call-done), channel_id=1, source_target_pairs={{0,4},{4,0},{1,5},{5,1},{2,6},{6,2},{3,7},{7,3},{8,12},{12,8},{9,1... | collective-permute-start | bytes 17301512 | tf_op jit(solution)/shard_map/ppermute | solution.py:338
  284.3 103.3 %collective-permute-start.3 = (bf16[1408,1024]{1,0:T(8,128)(2,1)}, bf16[1408,1024]{1,0:T(8,128)(2,1)}, u32[]{:S(2)}, u32[]{:S(2)}) collective-permute-start(bf16[1408,1024]{1,0:T(8,128)(2,1)} %all-gather.13.cloned.1.call-done), channel_id=1, source_target_pairs={{0,4},{4,0},{1,5},{5,1},{2,6},{6,2},{3,7},{7,3},{8,12},{12,8},{9,1... | collective-permute-start | bytes 8650760 | tf_op jit(solution)/shard_map/ppermute | solution.py:338
  286.5 93.3 %all-to-all-start.4 = ((bf16[8,96,1024]{2,1,0:T(8,128)(2,1)}), bf16[8,96,1024]{2,1,0:T(8,128)(2,1)S(1)}, u32[]{:S(2)}, u32[]{:S(2)}) async-start(bf16[8,96,1024]{2,1,0:T(8,128)(2,1)} %bitcast.231), calls=%async_computation.4 | async-start | bytes 3145728 | tf_op jit(solution)/shard_map/all_to_all | solution.py:423
  341.3 44.3 %collective-permute-start.1 = (bf16[512,1024]{1,0:T(8,128)(2,1)}, bf16[512,1024]{1,0:T(8,128)(2,1)}, u32[]{:S(2)}, u32[]{:S(2)}) collective-permute-start(bf16[512,1024]{1,0:T(8,128)(2,1)} %all-gather.9.cloned.1.call-done), channel_id=1, source_target_pairs={{0,4},{4,0},{1,5},{5,1},{2,6},{6,2},{3,7},{7,3},{8,12},{12,8},{9,1... | collective-permute-start | bytes 3145736 | tf_op jit(solution)/shard_map/ppermute | solution.py:338
  379.7 30.3 %all-to-all-start.2 = ((bf16[4,512,256]{1,2,0:T(8,128)(2,1)}), bf16[4,512,256]{1,2,0:T(8,128)(2,1)S(1)}, u32[]{:S(2)}, u32[]{:S(2)}) async-start(bf16[4,512,256]{1,2,0:T(8,128)(2,1)} %copy.121), calls=%async_computation.2 | async-start | bytes 2097152 | tf_op jit(solution)/shard_map/all_to_all | solution.py:426
  459.8 30.5 %all-to-all-start.5 = ((bf16[4,512,256]{2,1,0:T(8,128)(2,1)}), bf16[4,512,256]{2,1,0:T(8,128)(2,1)}, u32[]{:S(2)}, u32[]{:S(2)}) async-start(bf16[4,512,256]{2,1,0:T(8,128)(2,1)} %bitcast.223), calls=%async_computation.5 | async-start | bytes 2097152 | tf_op jit(solution)/shard_map/all_to_all | solution.py:426
  554.0 43.6 %collective-permute-start.7 = (bf16[4,352,1024]{2,1,0:T(8,128)(2,1)}, bf16[4,352,1024]{2,1,0:T(8,128)(2,1)}, u32[]{:S(2)}, u32[]{:S(2)}) collective-permute-start(bf16[4,352,1024]{2,1,0:T(8,128)(2,1)} %fusion.17), channel_id=1, source_target_pairs={{0,4},{4,0},{1,5},{5,1},{2,6},{6,2},{3,7},{7,3},{8,12},{12,8},{9,1... | collective-permute-start | bytes 8650760 | tf_op jit(solution)/shard_map/ppermute | solution.py:338
  568.8 115.0 %reduce-scatter.13.cloned.1.call-start = ((), (), s32[]{:S(2)}) async-start(), calls=%async_computation.24 | async-start | bytes 1310720 | tf_op jit(solution)/shard_map/reduce_scatter | solution.py:365
  597.6 86.9 %reduce-scatter.21.cloned.1.call-start = ((), (), s32[]{:S(2)}) async-start(), calls=%async_computation.28 | async-start | bytes 3604480 | tf_op jit(solution)/shard_map/reduce_scatter | solution.py:365
  606.3 104.7 %reduce-scatter.9.cloned.1.call-start = ((), (), s32[]{:S(2)}) async-start(), calls=%async_computation.22 | async-start | bytes 3932160 | tf_op jit(solution)/shard_map/reduce_scatter | solution.py:365
  669.0 128.0 %reduce-scatter.17.cloned.1.call-start = ((), (), s32[]{:S(2)}) async-start(), calls=%async_computation.26 | async-start | bytes 7208960 | tf_op jit(solution)/shard_map/reduce_scatter | solution.py:365
  683.7 142.8 %reduce-scatter.15.cloned.1.call-start = ((), (), s32[]{:S(2)}) async-start(), calls=%async_computation.25 | async-start | bytes 327680 | tf_op jit(solution)/shard_map/reduce_scatter | solution.py:366
  684.4 157.7 %reduce-scatter.23.cloned.1.call-start = ((), (), s32[]{:S(2)}) async-start(), calls=%async_computation.29 | async-start | bytes 901120 | tf_op jit(solution)/shard_map/reduce_scatter | solution.py:366
  685.0 181.8 %reduce-scatter.11.cloned.1.call-start = ((), (), s32[]{:S(2)}) async-start(), calls=%async_computation.23 | async-start | bytes 983040 | tf_op jit(solution)/shard_map/reduce_scatter | solution.py:366
  720.3 97.0 %all-to-all-start.3 = ((bf16[8,96,1024]{2,1,0:T(8,128)(2,1)}), bf16[8,96,1024]{2,1,0:T(8,128)(2,1)}, u32[]{:S(2)}, u32[]{:S(2)}) async-start(bf16[8,96,1024]{2,1,0:T(8,128)(2,1)} %bitcast.227), calls=%async_computation.3 | async-start | bytes 3145728 | tf_op jit(solution)/shard_map/all_to_all | solution.py:423
  724.7 176.8 %reduce-scatter.19.cloned.1.call-start = ((), (), s32[]{:S(2)}) async-start(), calls=%async_computation.27 | async-start | bytes 1802240 | tf_op jit(solution)/shard_map/reduce_scatter | solution.py:366
  817.3 101.8 %all-to-all-start.9 = ((bf16[8,96,1024]{2,1,0:T(8,128)(2,1)}), bf16[8,96,1024]{2,1,0:T(8,128)(2,1)S(1)}, u32[]{:S(2)}, u32[]{:S(2)}) async-start(bf16[8,96,1024]{2,1,0:T(8,128)(2,1)} %bitcast.216), calls=%async_computation.9 | async-start | bytes 3145728 | tf_op jit(solution)/shard_map/all_to_all | solution.py:423
  (60 other events, 1366.5 us)
Sparse Core Ops, SparseCore 0:
  11.5 70.7 all-gather.6
  85.5 93.3 all-gather.10
  182.2 102.0 all-gather.12
  287.4 53.7 all-gather.8
  572.8 28.1 reduce-scatter.12
  606.4 42.2 reduce-scatter.20
  669.1 41.8 reduce-scatter.8
  714.2 82.6 reduce-scatter.16
  799.3 19.5 reduce-scatter.14
  821.0 21.0 reduce-scatter.22
  844.4 22.3 reduce-scatter.10
  869.0 32.5 reduce-scatter.18
